TPU v7x, 512 devices: a whole 4x8x8 slice. The times are simulated.
512 devices in a mesh: chan: 16 (over z, core), exp: 32 (over x, y).
Axes of the slice: x: 4, y: 8, z: 8, core: 2. Of those that a mesh axis runs over, the one named last changes fastest.
Arguments:
- tokens: bfloat16 [96, 256, 2048], P('chan', 'exp'), may hold values from -6 to 6
- kernel: float32 [3, 3, 2048], replicated, may hold values from -2 to 2
- gain: float32 [2048], replicated, may hold values from 0.1 to 1.9
- routes: int32 [24576, 2], P(('chan', 'exp')), may hold values from 0 to 63, all different within a row; in each aligned block of 48 rows (0 to 47, 48 to 95, ...) at most 2 rows name the same one
- gate_num: int32 [24576, 2], P(('chan', 'exp')), may hold values from 1 to 15
- gate_proj: bfloat16 [512, 176, 2048], P(('exp', 'chan')), may hold values from -0.125 to 0.125
- up_proj: bfloat16 [512, 176, 2048], P(('exp', 'chan')), may hold values from -0.125 to 0.125
- down_proj: bfloat16 [512, 176, 2048], P(('exp', 'chan')), may hold values from -0.15625 to 0.15625
Outputs:
- mixed: bfloat16 [96, 256, 2048], P('chan', 'exp')
Inputs may be any that keep to these rules, and one draw needn't show every extreme that they name: `routes`: the two ids of a row differ. Rows r * 48 to r * 48 + 47 are the tokens of one device, and in each such block no expert is named more than 2 times; some expert is named exactly 2 times in some blocks.
All inputs are finite; a program needn't handle non-finite values.
Results may differ from a plain program's by a relative error of at most 0.0085.
Values may be sent and summed in bfloat16 or wider, within the bound.
A program may use at most 64 MiB of HBM per device.

v0:
```python
import jax
import jax.numpy as jnp
from jax import lax
from jax.sharding import PartitionSpec as P

EXP_DEV = 2


eps = 1e-06


def with_halo(block, sides, width):
    for axis, dim in sides:
        count = lax.axis_size(axis)
        forward = [(i, i + 1) for i in range(count - 1)]
        backward = [(target, source) for source, target in forward]
        low = lax.ppermute(
            lax.slice_in_dim(block, block.shape[dim] - width, None, axis=dim), axis, forward
        )
        high = lax.ppermute(lax.slice_in_dim(block, 0, width, axis=dim), axis, backward)
        block = jnp.concatenate([low, block, high], axis=dim)
    return block


def depthwise(padded, kernel, row_count, col_count):
    image = padded.astype(jnp.float32)
    conv_sum = jnp.zeros((row_count, col_count, image.shape[2]), jnp.float32)
    for row_shift in range(3):
        for col_shift in range(3):
            conv_sum = (
                conv_sum
                + kernel[row_shift, col_shift]
                * image[row_shift : row_shift + row_count, col_shift : col_shift + col_count]
            )
    return conv_sum


def body(tokens, kernel, gain, routes, gate_num, gate_proj, up_proj, down_proj):
    row_count, col_count, width = tokens.shape
    padded = with_halo(tokens, (("chan", 0), ("exp", 1)), 1)
    conv_out = depthwise(padded, kernel, row_count, col_count)
    local_tokens = row_count * col_count
    flat_conv = conv_out.reshape(local_tokens, width)
    inverse_rms = lax.rsqrt(jnp.mean(flat_conv * flat_conv, axis=1, keepdims=True) + eps)
    normed = (flat_conv * inverse_rms * gain).astype(jnp.bfloat16)
    owners = lax.axis_size("exp")
    chan_count = lax.axis_size("chan")
    expert_count = EXP_DEV * owners
    capacity = 3 * local_tokens // expert_count
    slices = chan_count // EXP_DEV
    slot_count = expert_count * capacity
    route_pairs = routes.reshape(-1)
    onehot = (route_pairs[:, None] == jnp.arange(expert_count, dtype=jnp.int32)[None, :]).astype(
        jnp.int32
    )
    earlier = jnp.cumsum(onehot, axis=0) - onehot
    slot_rank = jnp.sum(earlier * onehot, axis=1)
    slot_index = (route_pairs % EXP_DEV * owners + route_pairs // EXP_DEV) * capacity + slot_rank
    chosen = (slot_index[:, None] == jnp.arange(slot_count, dtype=jnp.int32)[None, :]).reshape(
        local_tokens, 2, slot_count
    )
    placing = jnp.sum(chosen.astype(jnp.bfloat16), axis=1)
    outgoing = lax.dot_general(
        placing, normed, (((0,), (0,)), ((), ())), preferred_element_type=jnp.float32
    )
    outgoing = outgoing.astype(jnp.bfloat16).reshape(EXP_DEV, owners, capacity, width)
    arrived = lax.all_to_all(outgoing, "exp", split_axis=1, concat_axis=1, tiled=True)
    half_index = lax.axis_index("chan") // slices
    own_rows = lax.dynamic_index_in_dim(
        lax.all_gather(arrived, "chan", axis=1, tiled=True), half_index, 0, keepdims=False
    )
    block_shape = own_rows.shape
    flat_rows = own_rows.reshape(-1, width)
    gate_val = lax.dot_general(
        flat_rows, gate_proj[0], (((1,), (1,)), ((), ())), preferred_element_type=jnp.float32
    )
    up_val = lax.dot_general(
        flat_rows, up_proj[0], (((1,), (1,)), ((), ())), preferred_element_type=jnp.float32
    )
    hidden = (jax.nn.silu(gate_val) * up_val).astype(jnp.bfloat16)
    down_part = jnp.dot(hidden, down_proj[0], preferred_element_type=jnp.float32).astype(
        jnp.bfloat16
    )
    partial_rows = down_part.reshape(block_shape)
    partial_rows = partial_rows.reshape(chan_count, owners, capacity, width)
    returned = lax.all_to_all(partial_rows, "chan", split_axis=0, concat_axis=0, tiled=True)
    summed = jnp.sum(
        returned.reshape(EXP_DEV, slices, owners, capacity, width).astype(jnp.float32), axis=1
    ).astype(jnp.bfloat16)
    returned_rows = lax.all_to_all(summed, "exp", split_axis=1, concat_axis=1, tiled=True)
    numer = gate_num.astype(jnp.float32)
    fraction = numer / jnp.sum(numer, axis=1, keepdims=True)
    weighting = jnp.sum(chosen.astype(jnp.float32) * fraction[:, :, None], axis=1)
    moe_out = jnp.dot(
        weighting,
        returned_rows.reshape(slot_count, width).astype(jnp.float32),
        precision=lax.Precision.HIGHEST,
    )
    mixed = (flat_conv + moe_out).astype(jnp.bfloat16)
    return mixed.reshape(row_count, col_count, width)


def solution(mesh):
    return jax.shard_map(
        body,
        mesh=mesh,
        in_specs=(
            P("chan", "exp", None),
            P(),
            P(),
            P(("chan", "exp"), None),
            P(("chan", "exp"), None),
            P(("exp", "chan"), None, None),
            P(("exp", "chan"), None, None),
            P(("exp", "chan"), None, None),
        ),
        out_specs=P("chan", "exp", None),
        check_vma=False,
    )
```

profile of v0, /device:TPU:9, one launch (start us, length us, event | category | flops | bytes accessed | tf_op | source)
XLA Modules:
  0.0 289.5 jit_solution(8126721402879814620)
XLA Ops:
  6.5 0.9 fusion.41
  7.4 4.5 %collective-permute-start = (bf16[1,8,2048]{2,1,0:T(8,128)(2,1)S(1)}, bf16[1,8,2048]{2,1,0:T(8,128)(2,1)S(1)}, u32[]{:S(2)}, u32[]{:S(2)}) collective-permute-start(bf16[1,8,2048]{2,1,0:T(8,128)(2,1)S(1)} %get-tuple-element.10), channel_id=1, source_target_pairs={{0,32},{32,64},{64,96},{96,128},{128,160},{160,192},{192,224},{224... | collective-permute-start | bytes 98312 | tf_op jit(solution)/shard_map/ppermute | solution.py:17
  12.0 1.9 collective-permute-start.1
  13.9 0.8 copy.61
  14.7 0.7 broadcast_compare_fusion
  15.3 1.0 fusion.42
  17.3 0.9 constant_dynamic-update-slice_fusion.1
  18.3 3.2 %collective-permute-start.2 = (bf16[8,1,2048]{2,1,0:T(2,128)(2,1)S(1)}, bf16[8,1,2048]{2,1,0:T(2,128)(2,1)S(1)}, u32[]{:S(2)}, u32[]{:S(2)}) collective-permute-start(bf16[8,1,2048]{2,1,0:T(2,128)(2,1)S(1)} %get-tuple-element.7), channel_id=1, source_target_pairs={{0,1},{1,2},{2,3},{3,4},{4,5},{5,6},{6,7},{7,8},{8,9},{9,10},{10,1... | collective-permute-start | bytes 98312 | tf_op jit(solution)/shard_map/ppermute | solution.py:17
  21.6 2.9 %collective-permute-start.3 = (bf16[8,1,2048]{2,1,0:T(2,128)(2,1)S(1)}, bf16[8,1,2048]{2,1,0:T(2,128)(2,1)S(1)}, u32[]{:S(2)}, u32[]{:S(2)}) collective-permute-start(bf16[8,1,2048]{2,1,0:T(2,128)(2,1)S(1)} %get-tuple-element.8), channel_id=1, source_target_pairs={{1,0},{2,1},{3,2},{4,3},{5,4},{6,5},{7,6},{8,7},{9,8},{10,9},{11,1... | collective-permute-start | bytes 98312 | tf_op jit(solution)/shard_map/ppermute | solution.py:20
  24.8 1.8 collective-permute-done.3
  26.8 0.6 multiply_reduce_fusion
  28.8 27.3 %all_to_all.15 = bf16[2,32,2,2048]{3,2,0,1:T(2,128)(2,1)} all-to-all(bf16[2,32,2,2048]{3,2,0,1:T(2,128)(2,1)S(1)} %copy.69), channel_id=1, replica_groups=mesh['chan'=16,'exp'=32] {'exp'}, dimensions={1} | all-to-all | bytes 1048576 | tf_op jit(solution)/shard_map/all_to_all | solution.py:67
  56.1 58.8 %all-gather.2.cloned.1.call-done = bf16[2,512,2,2048]{3,2,0,1:T(2,128)(2,1)} async-done(((bf16[2,32,2,2048]{3,2,0,1:T(2,128)(2,1)}), bf16[2,512,2,2048]{3,2,0,1:T(2,128)(2,1)}) %all-gather.2.cloned.1.call-update) | async-done | bytes 8388624 | tf_op jit(solution)/shard_map/all_gather | solution.py:70
  115.0 7.0 %constant_dynamic-slice_fusion = bf16[1,512,2,2048]{3,2,0,1:T(2,128)(2,1)} fusion(bf16[2,512,2,2048]{3,2,0,1:T(2,128)(2,1)} %all-gather.2.cloned.1.call-done, s32[]{:T(128)S(6)} %select_n.31), kind=kLoop, calls=%fused_computation.70 | loop fusion | bytes 8388612 | tf_op jit(solution)/shard_map/jit(dynamic_index_in_dim)/dynamic_slice | solution.py:69
  122.0 7.3 %reshape.100 = bf16[1024,2048]{1,0:T(8,128)(2,1)} reshape(bf16[1,512,2,2048]{3,2,0,1:T(2,128)(2,1)} %constant_dynamic-slice_fusion) | data formatting | bytes 8388608 | tf_op jit(solution)/shard_map/reshape | solution.py:73
  129.3 4.7 %fusion.6 = f32[1024,176]{0,1:T(8,128)} fusion(bf16[1024,2048]{1,0:T(8,128)(2,1)} %reshape.100, bf16[1,176,2048]{2,1,0:T(8,128)(2,1)S(1)} %copy-done.3), kind=kOutput, calls=%fused_computation.10 | convolution fusion | flops 738197504 | bytes 5636096 | tf_op jit(solution)/shard_map/dot_general | solution.py:74
  134.0 7.1 %convolution_convert_fusion = bf16[1024,2048]{1,0:T(8,128)(2,1)} fusion(bf16[1024,2048]{1,0:T(8,128)(2,1)} %reshape.100, bf16[1,176,2048]{2,1,0:T(8,128)(2,1)S(1)} %copy-done, bf16[1,176,2048]{2,1,0:T(8,128)(2,1)S(1)} %copy-done.4, f32[1024,176]{0,1:T(8,128)} %fusion.6), kind=kOutput, calls=%fused_computation.1 | convolution fusion | flops 1479573504 | bytes 10551296 | tf_op jit(solution)/shard_map/dot_general | solution.py:81
  141.1 7.6 %reshape_reshape.3 = bf16[16,32,2,2048]{3,2,1,0:T(2,128)(2,1)} reshape(bf16[1024,2048]{1,0:T(8,128)(2,1)} %convolution_convert_fusion) | data formatting | bytes 8388608 | tf_op jit(solution)/shard_map/reshape;reshape | solution.py:85
  148.7 100.3 %all_to_all.16 = bf16[16,32,2,2048]{3,2,1,0:T(2,128)(2,1)S(1)} all-to-all(bf16[16,32,2,2048]{3,2,1,0:T(2,128)(2,1)} %reshape_reshape.3), channel_id=1, replica_groups=mesh['chan'=16,'exp'=32] {'chan'}, dimensions={0} | all-to-all | bytes 8388608 | tf_op jit(solution)/shard_map/all_to_all | solution.py:86
  249.0 3.8 %bitcast_reduce_fusion = bf16[2,32,2,2048]{3,2,1,0:T(2,128)(2,1)S(1)} fusion(bf16[16,32,2,2048]{3,2,1,0:T(2,128)(2,1)S(1)} %all_to_all.16), kind=kLoop, calls=%fused_computation | loop fusion | flops 1835008 | bytes 4718592 | tf_op jit(solution)/shard_map/reduce_sum | solution.py:87
  252.9 1.4 copy.70
  254.2 9.3 %all-to-all-start.2 = ((bf16[2,32,2,2048]{3,2,0,1:T(2,128)(2,1)}), bf16[2,32,2,2048]{3,2,0,1:T(2,128)(2,1)S(1)}, u32[]{:S(2)}, u32[]{:S(2)}) async-start(bf16[2,32,2,2048]{3,2,0,1:T(2,128)(2,1)} %copy.70), calls=%async_computation.2 | async-start | bytes 1048576 | tf_op jit(solution)/shard_map/all_to_all | solution.py:90
  263.6 17.4 %all-to-all-done.2 = bf16[2,32,2,2048]{3,2,0,1:T(2,128)(2,1)S(1)} async-done(((bf16[2,32,2,2048]{3,2,0,1:T(2,128)(2,1)}), bf16[2,32,2,2048]{3,2,0,1:T(2,128)(2,1)S(1)}, u32[]{:S(2)}, u32[]{:S(2)}) %all-to-all-start.2) | async-done | bytes 524320 | tf_op jit(solution)/shard_map/all_to_all | solution.py:90
  281.6 1.0 fusion.1
  (38 shorter events, 3.5 us)
Async XLA Ops:
  6.5 127.5 %copy-start = (bf16[1,176,2048]{2,1,0:T(8,128)(2,1)S(1)}, bf16[1,176,2048]{2,1,0:T(8,128)(2,1)}, u32[]{:S(2)}) copy-start(bf16[1,176,2048]{2,1,0:T(8,128)(2,1)} %param.15) | copy-start | bytes 2162692
  6.5 21.0 %copy-start.1 = (f32[2048]{0:T(1024)S(1)}, f32[2048]{0:T(1024)}, u32[]{:S(2)}) copy-start(f32[2048]{0:T(1024)} %param.10) | copy-start | bytes 24580
  6.5 108.4 %all-gather.2.cloned.1.call-start = ((), (), s32[]{:S(2)}) async-start(), calls=%async_computation.3 | async-start | bytes 8912896 | tf_op jit(solution)/shard_map/all_gather | solution.py:70
  7.4 9.9 %collective-permute-start = (bf16[1,8,2048]{2,1,0:T(8,128)(2,1)S(1)}, bf16[1,8,2048]{2,1,0:T(8,128)(2,1)S(1)}, u32[]{:S(2)}, u32[]{:S(2)}) collective-permute-start(bf16[1,8,2048]{2,1,0:T(8,128)(2,1)S(1)} %get-tuple-element.10), channel_id=1, source_target_pairs={{0,32},{32,64},{64,96},{96,128},{128,160},{160,192},{192,224},{224... | collective-permute-start | bytes 98312 | tf_op jit(solution)/shard_map/ppermute | solution.py:17
  12.0 6.3 %collective-permute-start.1 = (bf16[1,8,2048]{2,1,0:T(8,128)(2,1)S(1)}, bf16[1,8,2048]{2,1,0:T(8,128)(2,1)S(1)}, u32[]{:S(2)}, u32[]{:S(2)}) collective-permute-start(bf16[1,8,2048]{2,1,0:T(8,128)(2,1)S(1)} %get-tuple-element.9), channel_id=1, source_target_pairs={{32,0},{64,32},{96,64},{128,96},{160,128},{192,160},{224,192},{256... | collective-permute-start | bytes 98312 | tf_op jit(solution)/shard_map/ppermute | solution.py:20
  18.3 6.4 %collective-permute-start.2 = (bf16[8,1,2048]{2,1,0:T(2,128)(2,1)S(1)}, bf16[8,1,2048]{2,1,0:T(2,128)(2,1)S(1)}, u32[]{:S(2)}, u32[]{:S(2)}) collective-permute-start(bf16[8,1,2048]{2,1,0:T(2,128)(2,1)S(1)} %get-tuple-element.7), channel_id=1, source_target_pairs={{0,1},{1,2},{2,3},{3,4},{4,5},{5,6},{6,7},{7,8},{8,9},{9,10},{10,1... | collective-permute-start | bytes 98312 | tf_op jit(solution)/shard_map/ppermute | solution.py:17
  21.6 5.0 %collective-permute-start.3 = (bf16[8,1,2048]{2,1,0:T(2,128)(2,1)S(1)}, bf16[8,1,2048]{2,1,0:T(2,128)(2,1)S(1)}, u32[]{:S(2)}, u32[]{:S(2)}) collective-permute-start(bf16[8,1,2048]{2,1,0:T(2,128)(2,1)S(1)} %get-tuple-element.8), channel_id=1, source_target_pairs={{1,0},{2,1},{3,2},{4,3},{5,4},{6,5},{7,6},{8,7},{9,8},{10,9},{11,1... | collective-permute-start | bytes 98312 | tf_op jit(solution)/shard_map/ppermute | solution.py:20
  122.0 7.3 %copy-start.3 = (bf16[1,176,2048]{2,1,0:T(8,128)(2,1)S(1)}, bf16[1,176,2048]{2,1,0:T(8,128)(2,1)}, u32[]{:S(2)}) copy-start(bf16[1,176,2048]{2,1,0:T(8,128)(2,1)} %param.13) | copy-start | bytes 2162692
  129.3 4.7 %copy-start.4 = (bf16[1,176,2048]{2,1,0:T(8,128)(2,1)S(1)}, bf16[1,176,2048]{2,1,0:T(8,128)(2,1)}, u32[]{:S(2)}) copy-start(bf16[1,176,2048]{2,1,0:T(8,128)(2,1)} %param.14) | copy-start | bytes 2162692
  249.0 14.5 %copy-start.2 = (s32[48,2]{0,1:T(2,128)S(1)}, s32[48,2]{0,1:T(2,128)}, u32[]{:S(2)}) copy-start(s32[48,2]{0,1:T(2,128)} %param.12) | copy-start | bytes 1156
  254.2 26.8 %all-to-all-start.2 = ((bf16[2,32,2,2048]{3,2,0,1:T(2,128)(2,1)}), bf16[2,32,2,2048]{3,2,0,1:T(2,128)(2,1)S(1)}, u32[]{:S(2)}, u32[]{:S(2)}) async-start(bf16[2,32,2,2048]{3,2,0,1:T(2,128)(2,1)} %copy.70), calls=%async_computation.2 | async-start | bytes 1048576 | tf_op jit(solution)/shard_map/all_to_all | solution.py:90
Sparse Core Ops, SparseCore 0:
  56.2 58.6 all-gather.1
where the time goes:
time: 290 us; the launch traced here: 289 us
  blocking collectives  128 us (44%)
  waiting for transfers between devices  78.2 us (27%)
  local copies, waits for them, and re-layouts  29 us (10%)
  starting transfers between devices  21.9 us (8%)
  between operations  13.6 us (5%)
  matrix products  13.2 us (5%)
  other arithmetic  5.98 us (2%)
    all_to_all x1, blocking collectives, body(): lax.all_to_all(partial_rows, 'chan', split_axis=0, concat_axis=0, tiled=T...  100 us
    all_gather x1, waiting for transfers between devices, body(): lax.all_gather(arrived, 'chan', axis=1, tiled=True)  58.8 us
    all_to_all x1, blocking collectives, body(): lax.all_to_all(outgoing, 'exp', split_axis=1, concat_axis=1, tiled=True)  27.3 us
    all_to_all x1, waiting for transfers between devices, body(): lax.all_to_all(summed, 'exp', split_axis=1, concat_axis=1, tiled=True)  17.4 us
    all_to_all x1, starting transfers between devices, body(): lax.all_to_all(summed, 'exp', split_axis=1, concat_axis=1, tiled=True)  9.28 us
    ppermute x2, starting transfers between devices, with_halo(): lax.ppermute(lax.slice_in_dim(block, block.shape[dim] - width, None, axis...  7.75 us
    another operation x1, local copies, waits for them, and re-layouts, body(): partial_rows = partial_rows.reshape(chan_count, owners, capacity, width)  7.62 us
    reshape x1, local copies, waits for them, and re-layouts, body(): flat_rows = own_rows.reshape(-1, width)  7.28 us
  transfers between devices with their start and end apart: 6, of which 4 were waited for; matrix products, arithmetic and copies ran while one was open for 2% of the time, Pallas kernels for 0%

commit v1 on v0

v1 whole, which is shorter than its diff:
```python
import jax
import jax.numpy as jnp
from jax import lax
from jax.experimental import pallas as pl
from jax.experimental.pallas import tpu as pltpu
from jax.sharding import PartitionSpec as P

D = 2048
FFS = 176
CB = 6
TB = 8
TOK = CB * TB
NX, NY, NZ = 4, 8, 8
HALF = NZ // 2
CAP = 2
SLOTS = 2 * NX * NY * CAP
F = 4
FW = D // F
ROWS = NZ * NX * NY * CAP
EPS = 1e-06
MESH = pl.DeviceIdType.MESH
f32 = jnp.float32
bf16 = jnp.bfloat16


def iota(shape, dim):
    return lax.broadcasted_iota(jnp.int32, shape, dim)


def kernel(
    tok, taps, gain, routes, numer, wg, wu, wd, out,
    pg, pu, pd, row_send, row_halo, col_send, col_halo, img, conv,
    o_buf, a1, b1, a2, x_buf, y_buf, r_buf, s_buf, t_buf, u_buf, q_buf,
    w_send, w_recv, h_send, h_recv, send, recv,
):
    c = lax.axis_index("chan")
    e = lax.axis_index("exp")
    n_chan = 2 * NZ
    n_exp = NX * NY
    z, core = c // 2, c % 2
    x, y = e // NY, e % NY
    half = z // HALF

    def y_dev(k):
        return (c, x * NY + (y + k) % NY)

    def x_dev(k):
        return (c, ((x + k) % NX) * NY + y)

    def z_dev(k):
        return (((z + k) % NZ) * 2 + core, e)

    c_low, c_high = (c + n_chan - 1) % n_chan, (c + 1) % n_chan
    e_low, e_high = (e + n_exp - 1) % n_exp, (e + 1) % n_exp

    barrier = pltpu.get_barrier_semaphore()

    def greet(device):
        pl.semaphore_signal(barrier, inc=1, device_id=device, device_id_type=MESH)

    for device in ((c_low, e), (c_high, e), (c, e_low), (c, e_high)):
        greet(device)
    for count, device_of in ((NY, y_dev), (NX, x_dev), (NZ, z_dev)):
        lax.fori_loop(1, count, lambda k, _, d=device_of: (greet(d(k)), 0)[1], 0)

    row_send[0] = tok[0].astype(f32)
    row_send[1] = tok[CB - 1].astype(f32)
    pl.semaphore_wait(barrier, 4 + NY - 1 + NX - 1 + NZ - 1)

    def copy(src, dst, s, r, device):
        return pltpu.make_async_remote_copy(
            src_ref=src, dst_ref=dst, send_sem=s, recv_sem=r, device_id=device, device_id_type=MESH
        )

    row_copies = [
        copy(row_send.at[0], row_halo.at[1], h_send.at[0], h_recv.at[0], (c_low, e)),
        copy(row_send.at[1], row_halo.at[0], h_send.at[1], h_recv.at[1], (c_high, e)),
    ]
    for one in row_copies:
        one.start()
    partner = (z * 2 + 1 - core, e)
    weight_copies = [
        copy(src.at[0], dst, w_send.at[i], w_recv.at[i], partner)
        for i, (src, dst) in enumerate(((wg, pg), (wu, pu), (wd, pd)))
    ]

    for i in range(CB):
        img[i + 1] = tok[i].astype(f32)

    col = iota((TOK, SLOTS), 1)
    col_expert = 2 * ((col // 2 % NX) * NY + col // 16) + col // 8 % 2
    named = [(routes[:, q : q + 1] == col_expert).astype(f32) for q in range(2)]
    before = (iota((TOK, TOK), 0) > iota((TOK, TOK), 1)).astype(bf16)
    earlier = jnp.dot(before, (named[0] + named[1]).astype(bf16), preferred_element_type=f32)
    in_slot = (earlier == (col % 2).astype(f32)).astype(f32)
    number = numer[...].astype(f32)
    placing = (in_slot * (named[0] + named[1])).astype(bf16)
    weighting = (
        in_slot * (named[0] * number[:, 0:1] + named[1] * number[:, 1:2])
    ).astype(bf16)
    weight_sum = number[:, 0:1] + number[:, 1:2]

    to = iota((SLOTS, SLOTS), 0)
    frm = iota((SLOTS, SLOTS), 1)
    by_x = (
        (to % 16) // 2 * 16 + to // 16 % 2 * 8 + to // 32 * 2 + to % 2 == frm
    ).astype(bf16)
    by_y = (
        to // 2 % 4 * 32 + to // 8 % 2 * 16 + to // 16 * 2 + to % 2 == frm
    ).astype(bf16)

    for one in row_copies:
        one.wait()
    img[0] = jnp.where(c == 0, 0.0, row_halo[0])
    img[CB + 1] = jnp.where(c == n_chan - 1, 0.0, row_halo[1])
    for i in range(CB + 2):
        col_send[0, i : i + 1] = img[i, 0:1]
        col_send[1, i : i + 1] = img[i, TB - 1 : TB]
    col_copies = [
        copy(col_send.at[0], col_halo.at[1], h_send.at[2], h_recv.at[2], (c, e_low)),
        copy(col_send.at[1], col_halo.at[0], h_send.at[3], h_recv.at[3], (c, e_high)),
    ]
    for one in col_copies:
        one.start()
    for one in weight_copies:
        one.start()
    for one in col_copies:
        one.wait()

    first, last = e == 0, e == n_exp - 1
    squares = jnp.zeros((TOK, 1), f32)
    place = iota((TB, FW), 0)
    for f in range(F):
        cols = slice(f * FW, (f + 1) * FW)
        rows = []
        for i in range(CB + 2):
            middle = img[i, :, cols]
            low = jnp.where(first, 0.0, col_halo[0, i : i + 1, cols])
            high = jnp.where(last, 0.0, col_halo[1, i : i + 1, cols])
            rows.append((
                jnp.where(place == 0, low, pltpu.roll(middle, 1, 0)),
                middle,
                jnp.where(place == TB - 1, high, pltpu.roll(middle, TB - 1, 0)),
            ))
        for i in range(CB):
            total = jnp.zeros((TB, FW), f32)
            for a in range(3):
                for b in range(3):
                    total = total + taps[a, b : b + 1, cols] * rows[i + a][b]
            conv[i * TB : (i + 1) * TB, cols] = total
        block = conv[:, cols]
        squares = squares + jnp.sum(block * block, axis=1, keepdims=True)
    inverse = lax.rsqrt(squares * (1.0 / D) + EPS)

    def start(stage, f, count, src, dst, device_of):
        def one(k, _):
            copy(src(k), dst, send.at[stage, f], recv.at[stage, f], device_of(k)).start()
            return 0

        lax.fori_loop(1, count, one, 0)

    def wait_recv(stage, f, ref):
        pltpu.make_async_copy(ref, ref, recv.at[stage, f]).wait()

    def wait_send(stage, f, ref):
        pltpu.make_async_copy(ref, ref, send.at[stage, f]).wait()

    for f in range(F):
        cols = slice(f * FW, (f + 1) * FW)
        normed = (conv[:, cols] * inverse * gain[:, cols]).astype(bf16)
        o_buf[f] = lax.dot_general(
            placing, normed, (((0,), (0,)), ((), ())), preferred_element_type=f32
        ).astype(bf16).reshape(NY, 16, FW)
        start(0, f, NY, lambda k: o_buf.at[f, (y + k) % NY], a1.at[f, y], y_dev)
        a1[f, y] = o_buf[f, y]

    def to_z(f):
        wait_recv(1, f, a2.at[f, :, pl.ds(0, NX - 1)])
        start(2, f, NZ, lambda k: a2.at[f, (z + k) % NZ // HALF], x_buf.at[f, z], z_dev)
        x_buf[f, z] = a2[f, half]

    for f in range(F):
        wait_recv(0, f, a1.at[f, pl.ds(0, NY - 1)])
        b1[f] = jnp.dot(
            by_x, a1[f].reshape(SLOTS, FW), preferred_element_type=f32
        ).astype(bf16).reshape(NX, 2, 16, FW)
        start(1, f, NX, lambda k: b1.at[f, (x + k) % NX], a2.at[f, :, x], x_dev)
        a2[f, :, x] = b1[f, x]
        if f:
            to_z(f - 1)
    to_z(F - 1)

    for one in weight_copies:
        one.wait()
    totals = [jnp.zeros((ROWS, FFS), f32) for _ in range(4)]
    for f in range(F):
        cols = slice(f * FW, (f + 1) * FW)
        wait_recv(2, f, x_buf.at[f, pl.ds(0, NZ - 1)])
        block = x_buf[f].reshape(ROWS, FW)
        for i, w in enumerate((wg[0, :, cols], wu[0, :, cols], pg[:, cols], pu[:, cols])):
            totals[i] = totals[i] + lax.dot_general(
                block, w, (((1,), (1,)), ((), ())), preferred_element_type=f32
            )
    hidden = [
        (g / (1.0 + jnp.exp(-g)) * u).astype(bf16)
        for g, u in ((totals[0], totals[1]), (totals[2], totals[3]))
    ]

    for f in range(F):
        cols = slice(f * FW, (f + 1) * FW)
        part = jnp.dot(hidden[0], wd[0, :, cols], preferred_element_type=f32)
        part = part + jnp.dot(hidden[1], pd[:, cols], preferred_element_type=f32)
        y_buf[f] = part.astype(bf16).reshape(NZ, NX, 16, FW)
        start(3, f, NZ, lambda k: y_buf.at[f, (z + k) % NZ], r_buf.at[f, z], z_dev)
        r_buf[f, z] = y_buf[f, z]

    def back_y(f):
        wait_recv(4, f, t_buf.at[f, pl.ds(0, NX - 1)])
        u_buf[f] = jnp.dot(
            by_y, t_buf[f].reshape(SLOTS, FW), preferred_element_type=f32
        ).astype(bf16).reshape(NY, 16, FW)
        start(5, f, NY, lambda k: u_buf.at[f, (y + k) % NY], q_buf.at[f, y], y_dev)
        q_buf[f, y] = u_buf[f, y]

    def finish(f):
        cols = slice(f * FW, (f + 1) * FW)
        wait_recv(5, f, q_buf.at[f, pl.ds(0, NY - 1)])
        moe = jnp.dot(weighting, q_buf[f].reshape(SLOTS, FW), preferred_element_type=f32)
        mixed = conv[:, cols] + moe / weight_sum
        for i in range(CB):
            out[i, :, cols] = mixed[i * TB : (i + 1) * TB].astype(bf16)

    for f in range(F):
        wait_recv(3, f, r_buf.at[f, pl.ds(0, NZ - 1)])
        for h in range(2):
            total = r_buf[f, h * HALF].astype(f32)
            for k in range(1, HALF):
                total = total + r_buf[f, h * HALF + k].astype(f32)
            s_buf[f, h] = total.astype(bf16)
        start(4, f, NX, lambda k: s_buf.at[f, :, (x + k) % NX], t_buf.at[f, x], x_dev)
        t_buf[f, x] = s_buf[f, :, x]
        if f:
            back_y(f - 1)
        if f > 1:
            finish(f - 2)
    back_y(F - 1)
    finish(F - 2)
    finish(F - 1)

    for f in range(F):
        wait_send(0, f, o_buf.at[f, pl.ds(0, NY - 1)])
        wait_send(1, f, b1.at[f, pl.ds(0, NX - 1)])
        wait_send(2, f, x_buf.at[f, pl.ds(0, NZ - 1)])
        wait_send(3, f, y_buf.at[f, pl.ds(0, NZ - 1)])
        wait_send(4, f, t_buf.at[f, pl.ds(0, NX - 1)])
        wait_send(5, f, u_buf.at[f, pl.ds(0, NY - 1)])


def body(tokens, taps, gain, routes, gate_num, gate_proj, up_proj, down_proj):
    vmem = pl.BlockSpec(memory_space=pltpu.VMEM)
    dma = pltpu.SemaphoreType.DMA
    return pl.pallas_call(
        kernel,
        out_shape=jax.ShapeDtypeStruct((CB, TB, D), bf16),
        in_specs=[vmem] * 8,
        out_specs=vmem,
        scratch_shapes=[
            pltpu.VMEM((FFS, D), bf16),
            pltpu.VMEM((FFS, D), bf16),
            pltpu.VMEM((FFS, D), bf16),
            pltpu.VMEM((2, TB, D), f32),
            pltpu.VMEM((2, TB, D), f32),
            pltpu.VMEM((2, TB, D), f32),
            pltpu.VMEM((2, TB, D), f32),
            pltpu.VMEM((CB + 2, TB, D), f32),
            pltpu.VMEM((TOK, D), f32),
            pltpu.VMEM((F, NY, 16, FW), bf16),
            pltpu.VMEM((F, NY, 16, FW), bf16),
            pltpu.VMEM((F, NX, 2, 16, FW), bf16),
            pltpu.VMEM((F, 2, NX, 16, FW), bf16),
            pltpu.VMEM((F, NZ, NX, 16, FW), bf16),
            pltpu.VMEM((F, NZ, NX, 16, FW), bf16),
            pltpu.VMEM((F, NZ, NX, 16, FW), bf16),
            pltpu.VMEM((F, 2, NX, 16, FW), bf16),
            pltpu.VMEM((F, NX, 2, 16, FW), bf16),
            pltpu.VMEM((F, NY, 16, FW), bf16),
            pltpu.VMEM((F, NY, 16, FW), bf16),
            dma((3,)),
            dma((3,)),
            dma((4,)),
            dma((4,)),
            dma((6, F)),
            dma((6, F)),
        ],
        compiler_params=pltpu.CompilerParams(
            collective_id=0, has_side_effects=True, vmem_limit_bytes=48 * 2**20
        ),
    )(tokens, taps, gain.reshape(1, D), routes, gate_num, gate_proj, up_proj, down_proj)


def solution(mesh):
    return jax.shard_map(
        body,
        mesh=mesh,
        in_specs=(
            P("chan", "exp", None),
            P(),
            P(),
            P(("chan", "exp"), None),
            P(("chan", "exp"), None),
            P(("exp", "chan"), None, None),
            P(("exp", "chan"), None, None),
            P(("exp", "chan"), None, None),
        ),
        out_specs=P("chan", "exp", None),
        check_vma=False,
    )
```

time: 290 us -> 147 us (0.51)
  the two profiles are of different devices: /device:TPU:9 before, /device:TPU:64 now
where the time goes in v1:
time: 147 us
  Pallas kernels  139 us (95%)
  local copies, waits for them, and re-layouts  7.88 us (5%)
    pallas_call x1, Pallas kernels, body(): pl.pallas_call(kernel, out_shape=jax.ShapeDtypeStruct((CB, TB, D), bf16),...  139 us
    unnamed x19, local copies, waits for them, and re-layouts  7.88 us

profile of v1, /device:TPU:64, one launch (start us, length us, event | category | flops | bytes accessed | tf_op | source)
XLA Modules:
  0.0 147.0 jit_solution(8409209419232491944)
XLA Ops:
  0.0 0.0 copy-start.6
  0.0 0.7 copy-done.6
  0.7 0.0 copy-start.7
  0.7 0.1 copy.9.routes
  0.8 0.6 copy-done.7
  1.4 0.0 copy-start.5
  1.4 0.1 copy.10.numer
  1.5 0.6 copy-done.5
  2.1 0.0 copy-start
  2.1 1.1 copy-done
  3.2 0.0 copy-start.1
  3.2 1.1 copy-done.1
  4.3 0.0 copy-start.2
  4.3 1.1 copy-done.2
  5.4 0.0 copy-start.3
  5.4 0.9 copy-done.3
  6.3 0.0 copy-start.4
  6.3 0.9 copy-done.4
  7.2 139.1 %shard_map.82 = bf16[6,8,2048]{2,1,0:T(8,128)(2,1)S(1)} custom-call(bf16[6,8,2048]{2,1,0:T(8,128)(2,1)S(1)} %copy-done.3, f32[3,3,2048]{2,1,0:T(4,128)S(1)} %copy-done.4, f32[1,2048]{1,0:T(1,128)S(1)} %bitcast.1, s32[48,2]{1,0:T(8,128)S(1)} %copy.9.routes, s32[48,2]{1,0:T(8,128)S(1)} %copy.10.numer, bf16[1,176,2048]{2,1,0:T(8,128)(2,1)S(1)} %copy-done, ...), custom_call_target="tpu_custom_call" | custom-call | tf_op jit(solution)/shard_map/pallas_call | solution.py:262
  146.3 0.7 copy.12
Async XLA Ops:
  0.0 0.7 copy-start.6
  0.7 0.7 copy-start.7
  1.4 0.7 copy-start.5
  2.1 1.1 copy-start
  3.2 1.1 copy-start.1
  4.3 1.1 copy-start.2
  5.4 0.9 copy-start.3
  6.3 0.9 copy-start.4

commit v2 on v1

v2 whole, which is shorter than its diff:
```python
import jax
import jax.numpy as jnp
from jax import lax
from jax.experimental import pallas as pl
from jax.experimental.pallas import tpu as pltpu
from jax.sharding import PartitionSpec as P

D = 2048
FFS = 176
CB = 6
TB = 8
TOK = CB * TB
NX, NY, NZ = 4, 8, 8
HALF = NZ // 2
CAP = 2
SLOTS = 2 * NX * NY * CAP
BLOCK = NX * NY * CAP
F = 4
FW = D // F
FH = FW // 2
FAR = 5
EPS = 1e-06
MESH = pl.DeviceIdType.MESH
f32 = jnp.float32
bf16 = jnp.bfloat16


def iota(shape, dim):
    return lax.broadcasted_iota(jnp.int32, shape, dim)


def loop(low, high, step):
    def one(k, carry):
        step(k)
        return carry

    lax.fori_loop(low, high, one, 0)


def kernel(
    tok_in, taps_in, gain_in, routes_in, numer_in, wg_in, wu_in, wd_in, out,
    tok, taps, gain, routes, numer, wg, wu, wd,
    pg, pu, pd, row_send, row_halo, col_send, col_halo, img, conv,
    o_buf, a1, b1, a2, x_buf, p_buf, r_buf, s_buf, t_buf, u_buf, q_buf,
    in_sem, w_send, w_recv, h_send, h_recv, y_send, y_recv, x_send, x_recv,
    go_send, go_recv, back_send, back_recv, xb_send, xb_recv, yb_send, yb_recv,
):
    c = lax.axis_index("chan")
    e = lax.axis_index("exp")
    n_chan = 2 * NZ
    n_exp = NX * NY
    z, core = c // 2, c % 2
    x, y = e // NY, e % NY
    half = z // HALF

    local = [
        pltpu.make_async_copy(src, dst, in_sem.at[i])
        for i, (src, dst) in enumerate((
            (tok_in, tok), (taps_in, taps), (routes_in, routes), (numer_in, numer),
            (gain_in, gain), (wg_in, wg), (wu_in, wu), (wd_in, wd),
        ))
    ]
    for one in local:
        one.start()

    def y_dev(k):
        return (c, x * NY + (y + k) % NY)

    def x_dev(k):
        return (c, ((x + k) % NX) * NY + y)

    def z_dev(k):
        return (((z + k + NZ) % NZ) * 2 + core, e)

    c_low, c_high = (c + n_chan - 1) % n_chan, (c + 1) % n_chan
    e_low, e_high = (e + n_exp - 1) % n_exp, (e + 1) % n_exp

    barrier = pltpu.get_barrier_semaphore()

    def greet(device):
        pl.semaphore_signal(barrier, inc=1, device_id=device, device_id_type=MESH)

    for device in (
        (c_low, e), (c_high, e), (c, e_low), (c, e_high), z_dev(1), z_dev(-1)
    ):
        greet(device)
    loop(1, NY, lambda k: greet(y_dev(k)))
    loop(1, NX, lambda k: greet(x_dev(k)))

    local[0].wait()
    row_send[0] = tok[0].astype(f32)
    row_send[1] = tok[CB - 1].astype(f32)
    for i in range(CB):
        img[i + 1] = tok[i].astype(f32)
    for one in local[1:5]:
        one.wait()

    before = (iota((TOK, TOK), 0) < iota((TOK, TOK), 1)).astype(bf16)

    def chosen(expert, cap):
        named = [(routes[q : q + 1] == expert).astype(f32) for q in range(2)]
        earlier = jnp.dot(
            (named[0] + named[1]).astype(bf16), before, preferred_element_type=f32
        )
        in_slot = (earlier == cap.astype(f32)).astype(f32)
        return in_slot * named[0], in_slot * named[1]

    slot = iota((SLOTS, TOK), 0)
    first, second = chosen(
        2 * ((slot // 2 % NX) * NY + slot // 16) + slot // 8 % 2, slot % 2
    )
    placing = (first + second).astype(bf16)
    number = numer[...].astype(f32)
    weighting = []
    for h in (half, 1 - half):
        first, second = chosen(2 * ((slot // 2 % NX) * NY + slot // 16) + h, slot % 2)
        both = first * number[0:1] + second * number[1:2]
        weighting.append([
            (both * (slot // 8 % 2 == part).astype(f32)).astype(bf16) for part in range(2)
        ])
    square = iota((TOK, TOK), 0) == iota((TOK, TOK), 1)
    weight_sum = jnp.sum(
        jnp.where(square, number[0:1] + number[1:2], 0.0), axis=1, keepdims=True
    )

    to = iota((SLOTS, SLOTS), 0)
    by_x = (
        to % 16 // 2 * 16 + to // 16 % 2 * 8 + to // 32 * 2 + to % 2 == iota((SLOTS, SLOTS), 1)
    ).astype(bf16)
    to = iota((SLOTS, BLOCK), 0)
    found = to // 2 % NX * 16 + to // 16 * 2 + to % 2 == iota((SLOTS, BLOCK), 1)
    by_y = [(found & (to // 8 % 2 == part)).astype(bf16) for part in range(2)]

    pl.semaphore_wait(barrier, 6 + NY - 1 + NX - 1)

    def copy(src, dst, s, r, device):
        return pltpu.make_async_remote_copy(
            src_ref=src, dst_ref=dst, send_sem=s, recv_sem=r, device_id=device, device_id_type=MESH
        )

    row_copies = [
        copy(row_send.at[0], row_halo.at[1], h_send.at[0], h_recv.at[0], (c_low, e)),
        copy(row_send.at[1], row_halo.at[0], h_send.at[1], h_recv.at[1], (c_high, e)),
    ]
    for one in row_copies:
        one.start()
    partner = (z * 2 + 1 - core, e)
    for one in local[5:]:
        one.wait()
    weight_copies = [
        copy(src.at[0], dst, w_send.at[i], w_recv.at[i], partner)
        for i, (src, dst) in enumerate(((wg, pg), (wu, pu), (wd, pd)))
    ]

    for one in row_copies:
        one.wait()
    img[0] = jnp.where(c == 0, 0.0, row_halo[0])
    img[CB + 1] = jnp.where(c == n_chan - 1, 0.0, row_halo[1])
    for i in range(CB + 2):
        col_send[0, i : i + 1] = img[i, 0:1]
        col_send[1, i : i + 1] = img[i, TB - 1 : TB]
    col_copies = [
        copy(col_send.at[0], col_halo.at[1], h_send.at[2], h_recv.at[2], (c, e_low)),
        copy(col_send.at[1], col_halo.at[0], h_send.at[3], h_recv.at[3], (c, e_high)),
    ]
    for one in col_copies:
        one.start()
    for one in weight_copies:
        one.start()
    for one in col_copies:
        one.wait()

    left_end, right_end = e == 0, e == n_exp - 1
    squares = jnp.zeros((TOK, 1), f32)
    place = iota((TB, FW), 0)
    for f in range(F):
        cols = slice(f * FW, (f + 1) * FW)
        rows = []
        for i in range(CB + 2):
            middle = img[i, :, cols]
            low = jnp.where(left_end, 0.0, col_halo[0, i : i + 1, cols])
            high = jnp.where(right_end, 0.0, col_halo[1, i : i + 1, cols])
            rows.append((
                jnp.where(place == 0, low, pltpu.roll(middle, 1, 0)),
                middle,
                jnp.where(place == TB - 1, high, pltpu.roll(middle, TB - 1, 0)),
            ))
        for i in range(CB):
            total = jnp.zeros((TB, FW), f32)
            for a in range(3):
                for b in range(3):
                    total = total + taps[a, b : b + 1, cols] * rows[i + a][b]
            conv[i * TB : (i + 1) * TB, cols] = total
        block = conv[:, cols]
        squares = squares + jnp.sum(block * block, axis=1, keepdims=True)
    inverse = lax.rsqrt(squares * (1.0 / D) + EPS)

    def wait_all(ref, sem):
        pltpu.make_async_copy(ref, ref, sem).wait()

    for f in range(F):
        cols = slice(f * FW, (f + 1) * FW)
        normed = (conv[:, cols] * inverse * gain[:, cols]).astype(bf16)
        o_buf[f] = jnp.dot(placing, normed, preferred_element_type=f32).astype(
            bf16
        ).reshape(NY, 16, FW)
        loop(1, NY, lambda k: copy(
            o_buf.at[f, (y + k) % NY], a1.at[f, y], y_send.at[f], y_recv.at[f], y_dev(k)
        ).start())
        a1[f, y] = o_buf[f, y]

    def chain(way):
        h, up = way // 2, way % 2
        u = (z + NZ - HALF * h) % NZ
        at = ((1 - 2 * up) * u + 3 * up + NZ) % NZ
        return h, up, at

    def source(h, up, s):
        return ((1 - 2 * up) * s + 3 * up + HALF * h + NZ) % NZ

    def go(h, up, s, f, src):
        way, zs = 2 * h + up, source(h, up, s)
        return copy(
            src, x_buf.at[h, zs, f], go_send.at[way, s - 1, f], go_recv.at[way, s - 1, f],
            z_dev(2 * up - 1),
        )

    def back(h, up, s, f, src):
        way, zs = 2 * h + up, source(h, up, s)
        return copy(
            src, r_buf.at[h, up, zs, f], back_send.at[way, s - 1, f], back_recv.at[way, s - 1, f],
            z_dev(1 - 2 * up),
        )

    def send_own(f):
        def step(way):
            h, up, at = chain(way)

            @pl.when((at >= 1) & (at <= FAR))
            def _():
                go(h, up, at, f, a2.at[f, h]).start()

        loop(0, 4, step)

    def pass_on(t):
        def step(i):
            f, way = i // 4, i % 4
            h, up, at = chain(way)
            s = at + t

            @pl.when(s <= FAR)
            def _():
                block = x_buf.at[h, source(h, up, s), f]
                go(h, up, s, f, block).wait_recv()

                @pl.when(at >= 1)
                def _():
                    go(h, up, s, f, block).start()

        loop(0, 4 * F, step)

    def first_back(s):
        def step(i):
            f, way = i // 4, i % 4
            h, up, at = chain(way)

            @pl.when(at == 0)
            def _():
                back(h, up, s, f, p_buf.at[source(h, up, s), f]).start()

        loop(0, 4 * F, step)

    def next_back(t):
        def step(i):
            f, way = i // 4, i % 4
            h, up, at = chain(way)
            s = t - at

            @pl.when((at >= 1) & (at <= s) & (s <= FAR))
            def _():
                zs = source(h, up, s)
                back(h, up, s, f, r_buf.at[h, up, zs, f]).wait_recv()

                @pl.when((at < HALF) & (at < s))
                def _():
                    r_buf[h, up, zs, f] = (
                        r_buf[h, up, zs, f].astype(f32) + p_buf[zs, f].astype(f32)
                    ).astype(bf16)

                @pl.when(at < s)
                def _():
                    back(h, up, s, f, r_buf.at[h, up, zs, f]).start()

        loop(0, 4 * F, step)

    def experts(blocks):
        size = BLOCK * len(blocks)
        totals = [jnp.zeros((size, FFS), f32) for _ in range(4)]
        for f in range(F):
            cols = slice(f * FW, (f + 1) * FW)
            rows = [x_buf[half, zs, f].reshape(BLOCK, FW) for zs in blocks]
            rows = rows[0] if len(rows) == 1 else jnp.concatenate(rows, axis=0)
            for i, w in enumerate((wg[0, :, cols], wu[0, :, cols], pg[:, cols], pu[:, cols])):
                totals[i] = totals[i] + lax.dot_general(
                    rows, w, (((1,), (1,)), ((), ())), preferred_element_type=f32
                )
        hidden = [
            (g / (1.0 + jnp.exp(-g)) * u).astype(bf16)
            for g, u in ((totals[0], totals[1]), (totals[2], totals[3]))
        ]
        for f in range(F):
            cols = slice(f * FW, (f + 1) * FW)
            part = jnp.dot(hidden[0], wd[0, :, cols], preferred_element_type=f32)
            part = part + jnp.dot(hidden[1], pd[:, cols], preferred_element_type=f32)
            for i, zs in enumerate(blocks):
                p_buf[zs, f] = part[i * BLOCK : (i + 1) * BLOCK].astype(bf16).reshape(
                    NX, 16, FW
                )

    def gathered(f):
        wait_all(a2.at[f, :, pl.ds(0, NX - 1)], x_recv.at[f])
        send_own(f)
        x_buf[half, z, f] = a2[f, half]

    for f in range(F):
        wait_all(a1.at[f, pl.ds(0, NY - 1)], y_recv.at[f])
        b1[f] = jnp.dot(
            by_x, a1[f].reshape(SLOTS, FW), preferred_element_type=f32
        ).astype(bf16).reshape(NX, 2, 16, FW)
        loop(1, NX, lambda k: copy(
            b1.at[f, (x + k) % NX], a2.at[f, :, x], x_send.at[f], x_recv.at[f], x_dev(k)
        ).start())
        a2[f, :, x] = b1[f, x]
        if f:
            gathered(f - 1)
    gathered(F - 1)
    for one in weight_copies:
        one.wait()

    def back_x(o):
        h = half if o == 0 else 1 - half
        for f in range(F):
            total = jnp.zeros((NX, 16, FW), f32)
            if o == 0:
                total = p_buf[z, f].astype(f32)
            for up in range(2):
                at = chain(2 * h + up)[2]
                there = (at >= 1) & (at <= FAR)
                total = total + jnp.where(there, r_buf[h, up, z, f].astype(f32), 0.0)
            s_buf[o, f] = total.astype(bf16)
            loop(1, NX, lambda k: copy(
                s_buf.at[o, f, (x + k) % NX], t_buf.at[o, f, x],
                xb_send.at[o, f], xb_recv.at[o, f], x_dev(k),
            ).start())
            t_buf[o, f, x] = s_buf[o, f, x]

    def back_y(o):
        for f in range(F):
            wait_all(t_buf.at[o, f, pl.ds(0, NX - 1)], xb_recv.at[o, f])
            rows = t_buf[o, f].reshape(BLOCK, FW)
            total = jnp.dot(by_y[0], rows[:, :FH], preferred_element_type=f32)
            total = total + jnp.dot(by_y[1], rows[:, FH:], preferred_element_type=f32)
            u_buf[o, f] = total.astype(bf16).reshape(NY, 16, FH)
            loop(1, NY, lambda k: copy(
                u_buf.at[o, f, (y + k) % NY], q_buf.at[o, f, y],
                yb_send.at[o, f], yb_recv.at[o, f], y_dev(k),
            ).start())
            q_buf[o, f, y] = u_buf[o, f, y]

    u = z % HALF
    near = u // 2

    def at_distance(up, t):
        at = u if up == 0 else 3 - u
        return source(half, up, at + t)

    def at_far(up, t):
        return source(half, up, (1 - 2 * up) * u + 3 * up + t)

    experts([z])
    for t in range(1, 2 * FAR + 1):
        if t <= FAR:
            pass_on(t)
            if t <= 2:
                experts([at_distance(0, t), at_distance(1, t)])
            elif t <= 4:
                experts([at_far(near, t)])
            if t == 3:

                @pl.when((u == 1) | (u == 2))
                def _():
                    experts([at_far(1 - near, 3)])

            if t == 5:

                @pl.when((u == 0) | (u == 3))
                def _():
                    experts([at_far(near, 5)])

            first_back(t)
        if t > 1:
            next_back(t)
        if t == 6:
            back_x(0)
        if t == 7:
            back_y(0)
    back_x(1)

    def sent(i):
        f, s, way = i % F, i // F % FAR + 1, i // (F * FAR)
        h, up, at = chain(way)

        @pl.when((at >= 1) & (at <= s))
        def _():
            go(h, up, s, f, a2.at[f, h]).wait_send()

        @pl.when(at < s)
        def _():
            back(h, up, s, f, p_buf.at[0, f]).wait_send()

    loop(0, 4 * FAR * F, sent)
    back_y(1)
    for f in range(F):
        wait_all(o_buf.at[f, pl.ds(0, NY - 1)], y_send.at[f])
        wait_all(a2.at[f, :, pl.ds(0, NX - 1)], x_send.at[f])
        for o in range(2):
            wait_all(t_buf.at[o, f, pl.ds(0, NX - 1)], xb_send.at[o, f])
        wait_all(q_buf.at[0, f, pl.ds(0, NY - 1)], yb_recv.at[0, f])
        wait_all(q_buf.at[1, f, pl.ds(0, NY - 1)], yb_recv.at[1, f])
        for part in range(2):
            cols = slice(f * FW + part * FH, f * FW + (part + 1) * FH)
            moe = jnp.zeros((TOK, FH), f32)
            for o in range(2):
                moe = moe + lax.dot_general(
                    weighting[o][part], q_buf[o, f].reshape(SLOTS, FH),
                    (((0,), (0,)), ((), ())), preferred_element_type=f32,
                )
            mixed = conv[:, cols] + moe / weight_sum
            for i in range(CB):
                out[i, :, cols] = mixed[i * TB : (i + 1) * TB].astype(bf16)
    for f in range(F):
        for o in range(2):
            wait_all(u_buf.at[o, f, pl.ds(0, NY - 1)], yb_send.at[o, f])


def body(tokens, taps, gain, routes, gate_num, gate_proj, up_proj, down_proj):
    anywhere = pl.BlockSpec(memory_space=pl.ANY)
    vmem = pltpu.VMEM
    dma = pltpu.SemaphoreType.DMA
    return pl.pallas_call(
        kernel,
        out_shape=jax.ShapeDtypeStruct((CB, TB, D), bf16),
        in_specs=[anywhere] * 8,
        out_specs=pl.BlockSpec(memory_space=pltpu.VMEM),
        scratch_shapes=[
            vmem((CB, TB, D), bf16),
            vmem((3, 3, D), f32),
            vmem((1, D), f32),
            vmem((2, TOK), jnp.int32),
            vmem((2, TOK), jnp.int32),
            vmem((1, FFS, D), bf16),
            vmem((1, FFS, D), bf16),
            vmem((1, FFS, D), bf16),
            vmem((FFS, D), bf16),
            vmem((FFS, D), bf16),
            vmem((FFS, D), bf16),
            vmem((2, TB, D), f32),
            vmem((2, TB, D), f32),
            vmem((2, TB, D), f32),
            vmem((2, TB, D), f32),
            vmem((CB + 2, TB, D), f32),
            vmem((TOK, D), f32),
            vmem((F, NY, 16, FW), bf16),
            vmem((F, NY, 16, FW), bf16),
            vmem((F, NX, 2, 16, FW), bf16),
            vmem((F, 2, NX, 16, FW), bf16),
            vmem((2, NZ, F, NX, 16, FW), bf16),
            vmem((NZ, F, NX, 16, FW), bf16),
            vmem((2, 2, NZ, F, NX, 16, FW), bf16),
            vmem((2, F, NX, 16, FW), bf16),
            vmem((2, F, NX, 16, FW), bf16),
            vmem((2, F, NY, 16, FH), bf16),
            vmem((2, F, NY, 16, FH), bf16),
            dma((8,)),
            dma((3,)),
            dma((3,)),
            dma((4,)),
            dma((4,)),
            dma((F,)),
            dma((F,)),
            dma((F,)),
            dma((F,)),
            dma((4, FAR, F)),
            dma((4, FAR, F)),
            dma((4, FAR, F)),
            dma((4, FAR, F)),
            dma((2, F)),
            dma((2, F)),
            dma((2, F)),
            dma((2, F)),
        ],
        compiler_params=pltpu.CompilerParams(
            collective_id=0, has_side_effects=True, vmem_limit_bytes=56 * 2**20
        ),
    )(
        tokens, taps, gain.reshape(1, D), routes.T, gate_num.T, gate_proj, up_proj, down_proj
    )


def solution(mesh):
    return jax.shard_map(
        body,
        mesh=mesh,
        in_specs=(
            P("chan", "exp", None),
            P(),
            P(),
            P(("chan", "exp"), None),
            P(("chan", "exp"), None),
            P(("exp", "chan"), None, None),
            P(("exp", "chan"), None, None),
            P(("exp", "chan"), None, None),
        ),
        out_specs=P("chan", "exp", None),
        check_vma=False,
    )
```

time: 147 us -> 114 us (0.78)
  Pallas kernels: 139 us -> 113 us
  local copies, waits for them, and re-layouts: 7.88 us -> 1.62 us
    pallas_call x1, Pallas kernels: 139 us -> 113 us  [body(): pl.pallas_call(kernel, out_shape=jax.ShapeDtypeStruct((CB, TB, D), bf16),...]
    unnamed x19 -> x1, local copies, waits for them, and re-layouts: 7.88 us -> 1.62 us
where the time goes in v2:
time: 114 us
  Pallas kernels  113 us (99%)
  local copies, waits for them, and re-layouts  1.62 us (1%)
    pallas_call x1, Pallas kernels, body(): pl.pallas_call(kernel, out_shape=jax.ShapeDtypeStruct((CB, TB, D), bf16),...  113 us

profile of v2, /device:TPU:64, one launch (start us, length us, event | category | flops | bytes accessed | tf_op | source)
XLA Modules:
  0.0 114.2 jit_solution(17920948850925917688)
XLA Ops:
  0.0 112.6 %shard_map.82 = bf16[6,8,2048]{2,1,0:T(8,128)(2,1)} custom-call(bf16[6,8,2048]{2,1,0:T(8,128)(2,1)} %tok_in.1, f32[3,3,2048]{2,1,0:T(4,128)} %taps_in.1, f32[1,2048]{1,0:T(1,128)} %bitcast.3, s32[2,48]{1,0:T(2,128)} %bitcast.4, s32[2,48]{1,0:T(2,128)} %bitcast.5, bf16[1,176,2048]{2,1,0:T(8,128)(2,1)} %wg_in.1, bf16[1,176,2048]{2,1,0:T(8,128)(2,1)} %wu_in.1, ...), custom_call_target="tpu_custom_call" | custom-call | tf_op jit(solution)/shard_map/pallas_call | solution.py:450
  112.6 1.6 %copy.10 = bf16[6,8,2048]{2,1,0:T(8,128)(2,1)} copy(bf16[6,8,2048]{2,1,0:T(8,128)(2,1)} %shard_map.82) | data formatting | bytes 393216

commit v3 on v2

--- a/solution.py
+++ b/solution.py
@@ -39,8 +39,8 @@
 
 def kernel(
     tok_in, taps_in, gain_in, routes_in, numer_in, wg_in, wu_in, wd_in, out,
-    tok, taps, gain, routes, numer, wg, wu, wd,
-    pg, pu, pd, row_send, row_halo, col_send, col_halo, img, conv,
+    tok, taps, gain, routes, numer, w_in, w_out,
+    row_send, row_halo, col_send, col_halo, end_send, end_halo, img, conv,
     o_buf, a1, b1, a2, x_buf, p_buf, r_buf, s_buf, t_buf, u_buf, q_buf,
     in_sem, w_send, w_recv, h_send, h_recv, y_send, y_recv, x_send, x_recv,
     go_send, go_recv, back_send, back_recv, xb_send, xb_recv, yb_send, yb_recv,
@@ -53,45 +53,95 @@
     x, y = e // NY, e % NY
     half = z // HALF
 
+    def y_dev(k):
+        return (c, x * NY + (y + k) % NY)
+
+    def x_dev(k):
+        return (c, ((x + k) % NX) * NY + y)
+
+    def z_dev(k):
+        return (((z + k + NZ) % NZ) * 2 + core, e)
+
+    c_low, c_high = (c + n_chan - 1) % n_chan, (c + 1) % n_chan
+    e_low, e_high = (e + n_exp - 1) % n_exp, (e + 1) % n_exp
+
+    barrier = pltpu.get_barrier_semaphore()
+
+    def greet(device):
+        pl.semaphore_signal(barrier, inc=1, device_id=device, device_id_type=MESH)
+
+    for device in (
+        (c_low, e), (c_high, e), (c, e_low), (c, e_high),
+        z_dev(1), z_dev(-1), z_dev(2), z_dev(-2),
+        (c_low, e_low), (c_low, e_high), (c_high, e_low), (c_high, e_high),
+    ):
+        greet(device)
+    loop(1, NY, lambda k: greet(y_dev(k)))
+    loop(1, NX, lambda k: greet(x_dev(k)))
+
     local = [
         pltpu.make_async_copy(src, dst, in_sem.at[i])
         for i, (src, dst) in enumerate((
             (tok_in, tok), (taps_in, taps), (routes_in, routes), (numer_in, numer),
-            (gain_in, gain), (wg_in, wg), (wu_in, wu), (wd_in, wd),
+            (gain_in, gain), (wg_in.at[0], w_in.at[0, 0]), (wu_in.at[0], w_in.at[1, 0]),
+            (wd_in.at[0], w_out.at[0]),
         ))
     ]
     for one in local:
         one.start()
 
-    def y_dev(k):
-        return (c, x * NY + (y + k) % NY)
-
-    def x_dev(k):
-        return (c, ((x + k) % NX) * NY + y)
-
-    def z_dev(k):
-        return (((z + k + NZ) % NZ) * 2 + core, e)
-
-    c_low, c_high = (c + n_chan - 1) % n_chan, (c + 1) % n_chan
-    e_low, e_high = (e + n_exp - 1) % n_exp, (e + 1) % n_exp
-
-    barrier = pltpu.get_barrier_semaphore()
-
-    def greet(device):
-        pl.semaphore_signal(barrier, inc=1, device_id=device, device_id_type=MESH)
-
-    for device in (
-        (c_low, e), (c_high, e), (c, e_low), (c, e_high), z_dev(1), z_dev(-1)
-    ):
-        greet(device)
-    loop(1, NY, lambda k: greet(y_dev(k)))
-    loop(1, NX, lambda k: greet(x_dev(k)))
-
+    for side in range(2):
+        for i in (0, CB + 1):
+            col_send[side, i : i + 1] = jnp.zeros((1, D), f32)
     local[0].wait()
-    row_send[0] = tok[0].astype(f32)
-    row_send[1] = tok[CB - 1].astype(f32)
     for i in range(CB):
-        img[i + 1] = tok[i].astype(f32)
+        block = tok[i].astype(f32)
+        img[i + 1] = block
+        for side, j in enumerate((0, TB - 1)):
+            col_send[side, i + 1 : i + 2] = block[j : j + 1]
+        for end in range(2):
+            if i == end * (CB - 1):
+                row_send[end] = block
+                for side, j in enumerate((0, TB - 1)):
+                    end_send[end, side] = block[j : j + 1]
+    pl.semaphore_wait(barrier, 12 + NY - 1 + NX - 1)
+
+    def copy(src, dst, s, r, device):
+        return pltpu.make_async_remote_copy(
+            src_ref=src, dst_ref=dst, send_sem=s, recv_sem=r, device_id=device, device_id_type=MESH
+        )
+
+    c_ends, e_ends = (c_low, c_high), (e_low, e_high)
+    halo_copies = []
+    for end in range(2):
+        for side in range(2):
+            i = 4 + 2 * end + side
+            halo_copies.append(copy(
+                end_send.at[end, side], end_halo.at[1 - end, 1 - side],
+                h_send.at[i], h_recv.at[i], (c_ends[end], e_ends[side]),
+            ))
+    for end in range(2):
+        halo_copies.append(copy(
+            row_send.at[end], row_halo.at[1 - end], h_send.at[end], h_recv.at[end],
+            (c_ends[end], e),
+        ))
+        halo_copies.append(copy(
+            col_send.at[end], col_halo.at[1 - end], h_send.at[2 + end], h_recv.at[2 + end],
+            (c, e_ends[end]),
+        ))
+    for one in halo_copies:
+        one.start()
+    partner = (z * 2 + 1 - core, e)
+    for one in local[5:]:
+        one.wait()
+    weight_copies = [
+        copy(src, dst, w_send.at[i], w_recv.at[i], partner)
+        for i, (src, dst) in enumerate((
+            (w_in.at[0, 0], w_in.at[0, 1]), (w_in.at[1, 0], w_in.at[1, 1]),
+            (w_out.at[0], w_out.at[1]),
+        ))
+    ]
+
     for one in local[1:5]:
         one.wait()
 
@@ -131,44 +181,15 @@
     found = to // 2 % NX * 16 + to // 16 * 2 + to % 2 == iota((SLOTS, BLOCK), 1)
     by_y = [(found & (to // 8 % 2 == part)).astype(bf16) for part in range(2)]
 
-    pl.semaphore_wait(barrier, 6 + NY - 1 + NX - 1)
-
-    def copy(src, dst, s, r, device):
-        return pltpu.make_async_remote_copy(
-            src_ref=src, dst_ref=dst, send_sem=s, recv_sem=r, device_id=device, device_id_type=MESH
-        )
-
-    row_copies = [
-        copy(row_send.at[0], row_halo.at[1], h_send.at[0], h_recv.at[0], (c_low, e)),
-        copy(row_send.at[1], row_halo.at[0], h_send.at[1], h_recv.at[1], (c_high, e)),
-    ]
-    for one in row_copies:
+    for one in weight_copies:
         one.start()
-    partner = (z * 2 + 1 - core, e)
-    for one in local[5:]:
-        one.wait()
-    weight_copies = [
-        copy(src.at[0], dst, w_send.at[i], w_recv.at[i], partner)
-        for i, (src, dst) in enumerate(((wg, pg), (wu, pu), (wd, pd)))
-    ]
-
-    for one in row_copies:
+    for one in halo_copies:
         one.wait()
     img[0] = jnp.where(c == 0, 0.0, row_halo[0])
     img[CB + 1] = jnp.where(c == n_chan - 1, 0.0, row_halo[1])
-    for i in range(CB + 2):
-        col_send[0, i : i + 1] = img[i, 0:1]
-        col_send[1, i : i + 1] = img[i, TB - 1 : TB]
-    col_copies = [
-        copy(col_send.at[0], col_halo.at[1], h_send.at[2], h_recv.at[2], (c, e_low)),
-        copy(col_send.at[1], col_halo.at[0], h_send.at[3], h_recv.at[3], (c, e_high)),
-    ]
-    for one in col_copies:
-        one.start()
-    for one in weight_copies:
-        one.start()
-    for one in col_copies:
-        one.wait()
+    for side in range(2):
+        col_halo[side, 0:1] = jnp.where(c == 0, 0.0, end_halo[0, side])
+        col_halo[side, CB + 1 : CB + 2] = jnp.where(c == n_chan - 1, 0.0, end_halo[1, side])
 
     left_end, right_end = e == 0, e == n_exp - 1
     squares = jnp.zeros((TOK, 1), f32)
@@ -209,109 +230,102 @@
         ).start())
         a1[f, y] = o_buf[f, y]
 
-    def chain(way):
-        h, up = way // 2, way % 2
-        u = (z + NZ - HALF * h) % NZ
-        at = ((1 - 2 * up) * u + 3 * up + NZ) % NZ
-        return h, up, at
+    u = z % HALF
+    places = (u, HALF - 1 - u)
+    near = u // 2
+    far = HALF + u + near * (HALF - 1 - 2 * u)
 
     def source(h, up, s):
         return ((1 - 2 * up) * s + 3 * up + HALF * h + NZ) % NZ
 
-    def go(h, up, s, f, src):
+    def go(h, up, s, f, src, hop=1):
         way, zs = 2 * h + up, source(h, up, s)
         return copy(
             src, x_buf.at[h, zs, f], go_send.at[way, s - 1, f], go_recv.at[way, s - 1, f],
-            z_dev(2 * up - 1),
+            z_dev((2 * up - 1) * hop),
         )
 
-    def back(h, up, s, f, src):
+    def back(h, up, s, f, src, hop=1):
         way, zs = 2 * h + up, source(h, up, s)
         return copy(
             src, r_buf.at[h, up, zs, f], back_send.at[way, s - 1, f], back_recv.at[way, s - 1, f],
-            z_dev(1 - 2 * up),
+            z_dev((1 - 2 * up) * hop),
         )
 
     def send_own(f):
-        def step(way):
-            h, up, at = chain(way)
-
-            @pl.when((at >= 1) & (at <= FAR))
+        go(1 - half, near, far, f, a2.at[f, 1 - half], far - HALF + 1).start()
+        for up, at in enumerate(places):
+
+            @pl.when(at >= 1)
             def _():
-                go(h, up, at, f, a2.at[f, h]).start()
-
-        loop(0, 4, step)
+                go(half, up, at, f, a2.at[f, half]).start()
 
     def pass_on(t):
-        def step(i):
-            f, way = i // 4, i % 4
-            h, up, at = chain(way)
-            s = at + t
-
-            @pl.when(s <= FAR)
-            def _():
-                block = x_buf.at[h, source(h, up, s), f]
-                go(h, up, s, f, block).wait_recv()
-
-                @pl.when(at >= 1)
+        def step(f):
+            for up, at in enumerate(places):
+                s = at + t
+
+                @pl.when(s <= FAR)
                 def _():
-                    go(h, up, s, f, block).start()
-
-        loop(0, 4 * F, step)
+                    block = x_buf.at[half, source(half, up, s), f]
+                    go(half, up, s, f, block).wait_recv()
+
+                    @pl.when(at >= 1)
+                    def _():
+                        go(half, up, s, f, block).start()
+
+        loop(0, F, step)
 
     def first_back(s):
-        def step(i):
-            f, way = i // 4, i % 4
-            h, up, at = chain(way)
+        for up, at in enumerate(places):
 
             @pl.when(at == 0)
             def _():
-                back(h, up, s, f, p_buf.at[source(h, up, s), f]).start()
-
-        loop(0, 4 * F, step)
+                zs = source(half, up, s)
+                loop(0, F, lambda f: back(half, up, s, f, p_buf.at[zs, f]).start())
 
     def next_back(t):
-        def step(i):
-            f, way = i // 4, i % 4
-            h, up, at = chain(way)
-            s = t - at
-
-            @pl.when((at >= 1) & (at <= s) & (s <= FAR))
-            def _():
-                zs = source(h, up, s)
-                back(h, up, s, f, r_buf.at[h, up, zs, f]).wait_recv()
-
-                @pl.when((at < HALF) & (at < s))
+        def step(f):
+            for up, at in enumerate(places):
+                s = t - at
+
+                @pl.when((at >= 1) & (at <= s) & (s <= FAR))
                 def _():
-                    r_buf[h, up, zs, f] = (
-                        r_buf[h, up, zs, f].astype(f32) + p_buf[zs, f].astype(f32)
-                    ).astype(bf16)
-
-                @pl.when(at < s)
-                def _():
-                    back(h, up, s, f, r_buf.at[h, up, zs, f]).start()
-
-        loop(0, 4 * F, step)
+                    zs = source(half, up, s)
+                    block = r_buf.at[half, up, zs, f]
+                    back(half, up, s, f, block).wait_recv()
+
+                    @pl.when(at < s)
+                    def _():
+                        r_buf[half, up, zs, f] = (
+                            r_buf[half, up, zs, f].astype(f32) + p_buf[zs, f].astype(f32)
+                        ).astype(bf16)
+                        hop = jnp.where(at == HALF - 1, s - at, 1)
+                        back(half, up, s, f, block, hop).start()
+
+        loop(0, F, step)
 
     def experts(blocks):
         size = BLOCK * len(blocks)
-        totals = [jnp.zeros((size, FFS), f32) for _ in range(4)]
+        gate = jnp.zeros((size, 2 * FFS), f32)
+        value = jnp.zeros((size, 2 * FFS), f32)
         for f in range(F):
             cols = slice(f * FW, (f + 1) * FW)
             rows = [x_buf[half, zs, f].reshape(BLOCK, FW) for zs in blocks]
             rows = rows[0] if len(rows) == 1 else jnp.concatenate(rows, axis=0)
-            for i, w in enumerate((wg[0, :, cols], wu[0, :, cols], pg[:, cols], pu[:, cols])):
-                totals[i] = totals[i] + lax.dot_general(
-                    rows, w, (((1,), (1,)), ((), ())), preferred_element_type=f32
+            gate, value = [
+                total + lax.dot_general(
+                    rows, w_in[i, :, :, cols].reshape(2 * FFS, FW),
+                    (((1,), (1,)), ((), ())), preferred_element_type=f32,
                 )
-        hidden = [
-            (g / (1.0 + jnp.exp(-g)) * u).astype(bf16)
-            for g, u in ((totals[0], totals[1]), (totals[2], totals[3]))
-        ]
+                for i, total in ((0, gate), (1, value))
+            ]
+        hidden = (gate / (1.0 + jnp.exp(-gate)) * value).astype(bf16)
         for f in range(F):
             cols = slice(f * FW, (f + 1) * FW)
-            part = jnp.dot(hidden[0], wd[0, :, cols], preferred_element_type=f32)
-            part = part + jnp.dot(hidden[1], pd[:, cols], preferred_element_type=f32)
+            part = jnp.dot(
+                hidden, w_out[:, :, cols].reshape(2 * FFS, FW), preferred_element_type=f32
+            )
             for i, zs in enumerate(blocks):
                 p_buf[zs, f] = part[i * BLOCK : (i + 1) * BLOCK].astype(bf16).reshape(
                     NX, 16, FW
@@ -338,16 +352,15 @@
         one.wait()
 
     def back_x(o):
-        h = half if o == 0 else 1 - half
         for f in range(F):
-            total = jnp.zeros((NX, 16, FW), f32)
             if o == 0:
                 total = p_buf[z, f].astype(f32)
-            for up in range(2):
-                at = chain(2 * h + up)[2]
-                there = (at >= 1) & (at <= FAR)
-                total = total + jnp.where(there, r_buf[h, up, z, f].astype(f32), 0.0)
-            s_buf[o, f] = total.astype(bf16)
+                for up, at in enumerate(places):
+                    total = total + jnp.where(at >= 1, r_buf[half, up, z, f].astype(f32), 0.0)
+                s_buf[o, f] = total.astype(bf16)
+            else:
+                back(1 - half, near, far, f, r_buf.at[1 - half, near, z, f]).wait_recv()
+                s_buf[o, f] = r_buf[1 - half, near, z, f]
             loop(1, NX, lambda k: copy(
                 s_buf.at[o, f, (x + k) % NX], t_buf.at[o, f, x],
                 xb_send.at[o, f], xb_recv.at[o, f], x_dev(k),
@@ -367,59 +380,52 @@
             ).start())
             q_buf[o, f, y] = u_buf[o, f, y]
 
-    u = z % HALF
-    near = u // 2
-
-    def at_distance(up, t):
-        at = u if up == 0 else 3 - u
+    def block_of(up, t):
+        at = up * (HALF - 1) + (1 - 2 * up) * u
         return source(half, up, at + t)
 
-    def at_far(up, t):
-        return source(half, up, (1 - 2 * up) * u + 3 * up + t)
-
     experts([z])
-    for t in range(1, 2 * FAR + 1):
+    for t in range(1, FAR + 4):
         if t <= FAR:
             pass_on(t)
-            if t <= 2:
-                experts([at_distance(0, t), at_distance(1, t)])
-            elif t <= 4:
-                experts([at_far(near, t)])
-            if t == 3:
-
-                @pl.when((u == 1) | (u == 2))
-                def _():
-                    experts([at_far(1 - near, 3)])
-
-            if t == 5:
-
-                @pl.when((u == 0) | (u == 3))
-                def _():
-                    experts([at_far(near, 5)])
-
+        next_back(t)
+        if t <= 2:
+            experts([block_of(0, t), block_of(1, t)])
+        elif t <= 4:
+            experts([block_of(near, t)])
+        if t == 3:
+
+            @pl.when((u == 1) | (u == 2))
+            def _():
+                experts([block_of(1 - near, t)])
+
+        if t == 5:
+
+            @pl.when((u == 0) | (u == 3))
+            def _():
+                experts([block_of(near, t)])
+
+        if t <= FAR:
             first_back(t)
-        if t > 1:
-            next_back(t)
         if t == 6:
             back_x(0)
         if t == 7:
             back_y(0)
     back_x(1)
-
-    def sent(i):
-        f, s, way = i % F, i // F % FAR + 1, i // (F * FAR)
-        h, up, at = chain(way)
-
-        @pl.when((at >= 1) & (at <= s))
-        def _():
-            go(h, up, s, f, a2.at[f, h]).wait_send()
-
-        @pl.when(at < s)
-        def _():
-            back(h, up, s, f, p_buf.at[0, f]).wait_send()
-
-    loop(0, 4 * FAR * F, sent)
     back_y(1)
+
+    loop(0, F, lambda f: go(1 - half, near, far, f, a2.at[f, 0]).wait_send())
+    for up, at in enumerate(places):
+        for s in range(1, FAR + 1):
+
+            @pl.when((at >= 1) & (at <= s))
+            def _():
+                loop(0, F, lambda f: go(half, up, s, f, a2.at[f, 0]).wait_send())
+
+            @pl.when(at < s)
+            def _():
+                loop(0, F, lambda f: back(half, up, s, f, p_buf.at[0, f]).wait_send())
+
     for f in range(F):
         wait_all(o_buf.at[f, pl.ds(0, NY - 1)], y_send.at[f])
         wait_all(a2.at[f, :, pl.ds(0, NX - 1)], x_send.at[f])
@@ -458,16 +464,14 @@
             vmem((1, D), f32),
             vmem((2, TOK), jnp.int32),
             vmem((2, TOK), jnp.int32),
-            vmem((1, FFS, D), bf16),
-            vmem((1, FFS, D), bf16),
-            vmem((1, FFS, D), bf16),
-            vmem((FFS, D), bf16),
-            vmem((FFS, D), bf16),
-            vmem((FFS, D), bf16),
+            vmem((2, 2, FFS, D), bf16),
+            vmem((2, FFS, D), bf16),
             vmem((2, TB, D), f32),
             vmem((2, TB, D), f32),
             vmem((2, TB, D), f32),
             vmem((2, TB, D), f32),
+            vmem((2, 2, 1, D), f32),
+            vmem((2, 2, 1, D), f32),
             vmem((CB + 2, TB, D), f32),
             vmem((TOK, D), f32),
             vmem((F, NY, 16, FW), bf16),
@@ -484,8 +488,8 @@
             dma((8,)),
             dma((3,)),
             dma((3,)),
-            dma((4,)),
-            dma((4,)),
+            dma((8,)),
+            dma((8,)),
             dma((F,)),
             dma((F,)),
             dma((F,)),

time: 114 us -> 108 us (0.947)
  Pallas kernels: 113 us -> 106 us
    pallas_call x1, Pallas kernels: 113 us -> 106 us  [body(): pl.pallas_call(kernel, out_shape=jax.ShapeDtypeStruct((CB, TB, D), bf16),...]
where the time goes in v3:
time: 108 us
  Pallas kernels  106 us (98%)
  local copies, waits for them, and re-layouts  1.62 us (2%)
    pallas_call x1, Pallas kernels, body(): pl.pallas_call(kernel, out_shape=jax.ShapeDtypeStruct((CB, TB, D), bf16),...  106 us

profile of v3, /device:TPU:64, one launch (start us, length us, event | category | flops | bytes accessed | tf_op | source)
XLA Modules:
  0.0 108.1 jit_solution(11824993440753417186)
XLA Ops:
  0.0 106.5 %shard_map.82 = bf16[6,8,2048]{2,1,0:T(8,128)(2,1)} custom-call(bf16[6,8,2048]{2,1,0:T(8,128)(2,1)} %tok_in.1, f32[3,3,2048]{2,1,0:T(4,128)} %taps_in.1, f32[1,2048]{1,0:T(1,128)} %bitcast.3, s32[2,48]{1,0:T(2,128)} %bitcast.4, s32[2,48]{1,0:T(2,128)} %bitcast.5, bf16[1,176,2048]{2,1,0:T(8,128)(2,1)} %wg_in.1, bf16[1,176,2048]{2,1,0:T(8,128)(2,1)} %wu_in.1, ...), custom_call_target="tpu_custom_call" | custom-call | tf_op jit(solution)/shard_map/pallas_call | solution.py:456
  106.5 1.6 %copy.10 = bf16[6,8,2048]{2,1,0:T(8,128)(2,1)} copy(bf16[6,8,2048]{2,1,0:T(8,128)(2,1)} %shard_map.82) | data formatting | bytes 393216

commit v4 on v3

--- a/solution.py
+++ b/solution.py
@@ -35,6 +35,11 @@
         return carry
 
     lax.fori_loop(low, high, one, 0)
+
+
+def spread(count, step):
+    for k in sorted(range(1, count), key=lambda k: (-min(k, count - k), k)):
+        step(k)
 
 
 def kernel(
@@ -225,7 +230,7 @@
         o_buf[f] = jnp.dot(placing, normed, preferred_element_type=f32).astype(
             bf16
         ).reshape(NY, 16, FW)
-        loop(1, NY, lambda k: copy(
+        spread(NY, lambda k: copy(
             o_buf.at[f, (y + k) % NY], a1.at[f, y], y_send.at[f], y_recv.at[f], y_dev(k)
         ).start())
         a1[f, y] = o_buf[f, y]
@@ -341,7 +346,7 @@
         b1[f] = jnp.dot(
             by_x, a1[f].reshape(SLOTS, FW), preferred_element_type=f32
         ).astype(bf16).reshape(NX, 2, 16, FW)
-        loop(1, NX, lambda k: copy(
+        spread(NX, lambda k: copy(
             b1.at[f, (x + k) % NX], a2.at[f, :, x], x_send.at[f], x_recv.at[f], x_dev(k)
         ).start())
         a2[f, :, x] = b1[f, x]
@@ -361,7 +366,7 @@
             else:
                 back(1 - half, near, far, f, r_buf.at[1 - half, near, z, f]).wait_recv()
                 s_buf[o, f] = r_buf[1 - half, near, z, f]
-            loop(1, NX, lambda k: copy(
+            spread(NX, lambda k: copy(
                 s_buf.at[o, f, (x + k) % NX], t_buf.at[o, f, x],
                 xb_send.at[o, f], xb_recv.at[o, f], x_dev(k),
             ).start())
@@ -374,7 +379,7 @@
             total = jnp.dot(by_y[0], rows[:, :FH], preferred_element_type=f32)
             total = total + jnp.dot(by_y[1], rows[:, FH:], preferred_element_type=f32)
             u_buf[o, f] = total.astype(bf16).reshape(NY, 16, FH)
-            loop(1, NY, lambda k: copy(
+            spread(NY, lambda k: copy(
                 u_buf.at[o, f, (y + k) % NY], q_buf.at[o, f, y],
                 yb_send.at[o, f], yb_recv.at[o, f], y_dev(k),
             ).start())
@@ -388,7 +393,6 @@
     for t in range(1, FAR + 4):
         if t <= FAR:
             pass_on(t)
-        next_back(t)
         if t <= 2:
             experts([block_of(0, t), block_of(1, t)])
         elif t <= 4:
@@ -407,6 +411,7 @@
 
         if t <= FAR:
             first_back(t)
+        next_back(t)
         if t == 6:
             back_x(0)
         if t == 7:

time: 108 us -> 105 us (0.972)
  Pallas kernels: 106 us -> 103 us
    pallas_call x1, Pallas kernels: 106 us -> 103 us  [body(): pl.pallas_call(kernel, out_shape=jax.ShapeDtypeStruct((CB, TB, D), bf16),...]
where the time goes in v4:
time: 105 us
  Pallas kernels  103 us (98%)
  local copies, waits for them, and re-layouts  1.62 us (2%)
    pallas_call x1, Pallas kernels, body(): pl.pallas_call(kernel, out_shape=jax.ShapeDtypeStruct((CB, TB, D), bf16),...  103 us

profile of v4, /device:TPU:64, one launch (start us, length us, event | category | flops | bytes accessed | tf_op | source)
XLA Modules:
  0.0 104.9 jit_solution(12817724041787794437)
XLA Ops:
  0.0 103.3 %shard_map.82 = bf16[6,8,2048]{2,1,0:T(8,128)(2,1)} custom-call(bf16[6,8,2048]{2,1,0:T(8,128)(2,1)} %tok_in.1, f32[3,3,2048]{2,1,0:T(4,128)} %taps_in.1, f32[1,2048]{1,0:T(1,128)} %bitcast.3, s32[2,48]{1,0:T(2,128)} %bitcast.4, s32[2,48]{1,0:T(2,128)} %bitcast.5, bf16[1,176,2048]{2,1,0:T(8,128)(2,1)} %wg_in.1, bf16[1,176,2048]{2,1,0:T(8,128)(2,1)} %wu_in.1, ...), custom_call_target="tpu_custom_call" | custom-call | tf_op jit(solution)/shard_map/pallas_call | solution.py:461
  103.3 1.6 %copy.10 = bf16[6,8,2048]{2,1,0:T(8,128)(2,1)} copy(bf16[6,8,2048]{2,1,0:T(8,128)(2,1)} %shard_map.82) | data formatting | bytes 393216

commit v5 on v4

--- a/solution.py
+++ b/solution.py
@@ -92,7 +92,7 @@
             (wd_in.at[0], w_out.at[0]),
         ))
     ]
-    for one in local:
+    for one in local[:5]:
         one.start()
 
     for side in range(2):
@@ -136,9 +136,9 @@
         ))
     for one in halo_copies:
         one.start()
+    for one in local[5:]:
+        one.start()
     partner = (z * 2 + 1 - core, e)
-    for one in local[5:]:
-        one.wait()
     weight_copies = [
         copy(src, dst, w_send.at[i], w_recv.at[i], partner)
         for i, (src, dst) in enumerate((
@@ -186,8 +186,6 @@
     found = to // 2 % NX * 16 + to // 16 * 2 + to % 2 == iota((SLOTS, BLOCK), 1)
     by_y = [(found & (to // 8 % 2 == part)).astype(bf16) for part in range(2)]
 
-    for one in weight_copies:
-        one.start()
     for one in halo_copies:
         one.wait()
     img[0] = jnp.where(c == 0, 0.0, row_halo[0])
@@ -235,6 +233,11 @@
         ).start())
         a1[f, y] = o_buf[f, y]
 
+    for one in local[5:]:
+        one.wait()
+    for one in weight_copies:
+        one.start()
+
     u = z % HALF
     places = (u, HALF - 1 - u)
     near = u // 2
@@ -258,12 +261,13 @@
         )
 
     def send_own(f):
+        for up, at in enumerate(places):
+
+            @pl.when(at >= 1)
+            def _():
+                go(half, up, at, f, a2.at[f, half]).start()
+
         go(1 - half, near, far, f, a2.at[f, 1 - half], far - HALF + 1).start()
-        for up, at in enumerate(places):
-
-            @pl.when(at >= 1)
-            def _():
-                go(half, up, at, f, a2.at[f, half]).start()
 
     def pass_on(t):
         def step(f):
@@ -389,6 +393,7 @@
         at = up * (HALF - 1) + (1 - 2 * up) * u
         return source(half, up, at + t)
 
+    ends = (u == 0) | (u == HALF - 1)
     experts([z])
     for t in range(1, FAR + 4):
         if t <= FAR:
@@ -412,10 +417,18 @@
         if t <= FAR:
             first_back(t)
         next_back(t)
-        if t == 6:
-            back_x(0)
-        if t == 7:
-            back_y(0)
+        if t in (4, 6):
+
+            @pl.when(ends == (t == 6))
+            def _():
+                back_x(0)
+
+        if t in (5, 7):
+
+            @pl.when(ends == (t == 7))
+            def _():
+                back_y(0)
+
     back_x(1)
     back_y(1)
 

time: 105 us -> 105 us (level)
  no operation moved by 1% of the time
where the time goes in v5:
time: 105 us
  Pallas kernels  104 us (99%)
  local copies, waits for them, and re-layouts  1.62 us (2%)
    pallas_call x1, Pallas kernels, body(): pl.pallas_call(kernel, out_shape=jax.ShapeDtypeStruct((CB, TB, D), bf16),...  104 us

profile of v5, /device:TPU:64, one launch (start us, length us, event | category | flops | bytes accessed | tf_op | source)
XLA Modules:
  0.0 105.3 jit_solution(13324746682156523670)
XLA Ops:
  0.0 103.7 %shard_map.82 = bf16[6,8,2048]{2,1,0:T(8,128)(2,1)} custom-call(bf16[6,8,2048]{2,1,0:T(8,128)(2,1)} %tok_in.1, f32[3,3,2048]{2,1,0:T(4,128)} %taps_in.1, f32[1,2048]{1,0:T(1,128)} %bitcast.3, s32[2,48]{1,0:T(2,128)} %bitcast.4, s32[2,48]{1,0:T(2,128)} %bitcast.5, bf16[1,176,2048]{2,1,0:T(8,128)(2,1)} %wg_in.1, bf16[1,176,2048]{2,1,0:T(8,128)(2,1)} %wu_in.1, ...), custom_call_target="tpu_custom_call" | custom-call | tf_op jit(solution)/shard_map/pallas_call | solution.py:474
  103.7 1.6 %copy.10 = bf16[6,8,2048]{2,1,0:T(8,128)(2,1)} copy(bf16[6,8,2048]{2,1,0:T(8,128)(2,1)} %shard_map.82) | data formatting | bytes 393216
